TPU v7x, 512 devices: a whole 4x8x8 slice. The times are simulated.
512 devices in a mesh: seq: 16 (over y, core), head: 32 (over z, x).
Axes of the slice: x: 4, y: 8, z: 8, core: 2. Of those that a mesh axis runs over, the one named last changes fastest.
Arguments:
- queries: bfloat16 [65536, 8192], P(('seq', 'head')), may hold values from -36 to 36
- keys_values: bfloat16 [65536, 2048], P(('seq', 'head')), may hold values from -14 to 14
- vertical: int32 [64, 4], replicated, may hold values from -1 to 63, as said below
- slash: int32 [64, 2], replicated, may hold values from -1 to 2, as said below
- assignment: int32 [64], replicated, may hold values from 0 to 63, as said below
Outputs:
- attended: bfloat16 [1024, 4096, 128], P(('seq', 'head'))
Inputs may be any that keep to these rules, and one draw needn't show every extreme that they name: `vertical`: row h lists distinct blocks below 64, used entries first and -1 after them; a row uses 1 to 4 entries. The rows of the 8 query heads of one key-value head name exactly 8 distinct blocks together. `slash`: row h lists distinct offsets, used entries first and -1 after them; a row uses 1 to 2 entries. `assignment`: every unit appears once. Slots 2 * d to 2 * d + 1 of a group belong to index d of the head axis, and their units are parts of query heads of one key-value head.
All inputs are finite; a program needn't handle non-finite values.
Results may differ from a plain program's by a relative error of at most 0.0065.
Values may be sent and summed in bfloat16 or wider, within the bound.
A program may use at most 64 MiB of HBM per device.

v0:
```python
import math
import jax
import jax.numpy as jnp
from jax import lax
from jax.sharding import PartitionSpec as P

HQ = 64
HK = 8
HD = 128
BLK = 64
REACH = 2
NV = 4
GQ = 8


def from_behind(value, axis, steps):
    count = lax.axis_size(axis)
    leading, last = (max(0, -steps), min(count, count - steps))
    return lax.ppermute(value, axis, [(source, source + steps) for source in range(leading, last)])


def broadcast(block, axis, holder):
    block = jnp.where(lax.axis_index(axis) == holder, block, jnp.zeros_like(block))
    return lax.psum(block, axis)


def softmax_update(state, scores, mask, product):
    top, total, accum = state
    masked = jnp.where(mask, scores, -jnp.inf)
    new_top = jnp.maximum(top, jnp.max(masked, axis=-1))
    factor = jnp.exp(top - new_top)
    weights = jnp.where(mask, jnp.exp(scores - new_top[..., None]), 0.0)
    total = total * factor + jnp.sum(weights, axis=-1)
    accum = accum * factor[..., None] + product(weights.astype(jnp.bfloat16))
    return (new_top, total, accum)


def attend_blocks(
    query_blocks,
    query_index,
    key_store,
    store_base,
    store_heads,
    vertical_store,
    vertical_slot,
    head_ids,
    vertical,
    slash,
):
    items, count, width, depth = query_blocks.shape
    scale = 1.0 / math.sqrt(depth)
    vert_rows = vertical[head_ids]
    slash_rows = slash[head_ids]
    main_steps = 1 + jnp.max(jnp.sum((slash_rows >= 1).astype(jnp.int32), axis=1))
    vertical_steps = jnp.max(jnp.sum((vert_rows >= 0).astype(jnp.int32), axis=1))
    stored = key_store.shape[0]
    causal = jnp.arange(width)[None, :] <= jnp.arange(width)[:, None]
    begin = (
        jnp.full((items, count, width), -jnp.inf, jnp.float32),
        jnp.zeros((items, count, width), jnp.float32),
        jnp.zeros((items, count, width, depth), jnp.float32),
    )

    def main_step(number, state):
        offset = jnp.where(number == 0, 0, jnp.take(slash_rows, jnp.maximum(number - 1, 0), axis=1))
        target = query_index - offset[:, None]
        repeated = jnp.any(target[:, :, None] == vert_rows[:, None, :], axis=-1)
        valid = (number == 0) | (offset[:, None] >= 1) & (target >= 0) & jnp.logical_not(repeated)
        local = jnp.clip(target - store_base, 0, stored - 1)
        fetched = key_store[local, :, store_heads[:, None]]
        keys = fetched[..., :depth]
        values = fetched[..., depth:]
        scores = (
            jnp.einsum("inqd,inkd->inqk", query_blocks, keys, preferred_element_type=jnp.float32)
            * scale
        )
        mask = valid[:, :, None, None] & ((number > 0) | causal)[None, None]
        return softmax_update(
            state,
            scores,
            mask,
            lambda weights: jnp.einsum(
                "inqk,inkd->inqd", weights, values, preferred_element_type=jnp.float32
            ),
        )

    def vertical_step(number, state):
        blocks = jnp.take(vert_rows, number, axis=1)
        valid = (blocks[:, None] >= 0) & (blocks[:, None] < query_index)
        fetched = vertical_store[jnp.take(vertical_slot, number, axis=1)]
        keys = fetched[..., :depth]
        values = fetched[..., depth:]
        scores = (
            jnp.einsum("inqd,ikd->inqk", query_blocks, keys, preferred_element_type=jnp.float32)
            * scale
        )
        mask = jnp.broadcast_to(valid[:, :, None, None], scores.shape)
        return softmax_update(
            state,
            scores,
            mask,
            lambda weights: jnp.einsum(
                "inqk,ikd->inqd", weights, values, preferred_element_type=jnp.float32
            ),
        )

    state = lax.fori_loop(0, main_steps, main_step, begin)
    state = lax.fori_loop(0, vertical_steps, vertical_step, state)
    top, total, accum = state
    return (accum / total[..., None]).astype(jnp.bfloat16)


def on_device(queries, keys_values, vertical, slash, assignment):
    rows = queries.shape[0]
    members = lax.axis_size("head")
    seq_place = lax.axis_index("seq")
    head_place = lax.axis_index("head")
    parts = max(1, 2 * members // HQ)
    per_device = parts * HQ // members
    portion = rows // parts
    device_blocks = rows // BLK
    group_blocks = device_blocks * members
    slot_major = assignment.reshape(members, per_device).T.reshape(-1)
    unit_heads = slot_major % HQ
    unit_parts = slot_major // HQ
    mine = lax.dynamic_slice_in_dim(assignment, per_device * head_place, per_device)
    my_heads = mine % HQ
    my_parts = mine // HQ
    split_queries = queries.reshape(parts, portion, HQ, HD)
    outgoing = split_queries[unit_parts, :, unit_heads].reshape(per_device, members, portion, HD)
    incoming = lax.all_to_all(outgoing, "head", split_axis=1, concat_axis=1, tiled=True)
    wanted = assignment.reshape(members, per_device)[:, 0] % HQ // GQ
    shipped = keys_values.reshape(rows, HK, 2 * HD)[:, wanted]
    group_pairs = lax.all_to_all(shipped, "head", split_axis=1, concat_axis=0, tiled=True)
    own_pairs = group_pairs[:, 0]
    group_tail = own_pairs[own_pairs.shape[0] - REACH * BLK :]
    before = from_behind(group_tail, "seq", 1)
    store_flat = jnp.concatenate([before, own_pairs], axis=0).reshape(
        REACH + group_blocks, BLK, 2 * HD
    )
    picked = store_flat[jnp.clip(vertical[my_heads], 0, None) + REACH]
    shared = broadcast(picked, "seq", 0)
    vertical_store = shared.reshape(per_device * NV, BLK, 2 * HD)
    per_portion = portion // BLK
    order = jnp.arange(members * per_portion, dtype=jnp.int32)
    query_index = (
        seq_place * group_blocks
        + (order // per_portion)[None, :] * device_blocks
        + my_parts[:, None] * per_portion
        + (order % per_portion)[None, :]
    )
    query_blocks = incoming.reshape(per_device, members * per_portion, BLK, HD)
    slot_rows = (
        jnp.arange(per_device, dtype=jnp.int32)[:, None] * NV
        + jnp.arange(NV, dtype=jnp.int32)[None, :]
    )
    outputs = attend_blocks(
        query_blocks,
        query_index,
        store_flat[:, :, None, :],
        seq_place * group_blocks - REACH,
        jnp.zeros((per_device,), jnp.int32),
        vertical_store,
        slot_rows,
        my_heads,
        vertical,
        slash,
    )
    attended = outputs.reshape(per_device, members * portion, HD)
    return attended


def solution(mesh):
    placed = (P(("seq", "head"), None), P(("seq", "head"), None), P(), P(), P())
    return jax.shard_map(
        on_device,
        mesh=mesh,
        in_specs=placed,
        out_specs=P(("seq", "head"), None, None),
        check_vma=False,
    )
```

profile of v0, /device:TPU:1, one launch (start us, length us, event | category | flops | bytes accessed | tf_op | source)
XLA Modules:
  0.0 312.2 jit_solution(15812212171097348099)
XLA Ops:
  6.5 0.7 reshape.378
  7.3 0.1 fusion.41
  7.4 1.3 copy.66
  8.8 0.2 copy.67
  9.0 2.0 gather_fusion.4
  11.0 13.7 %all-to-all-start = ((bf16[128,32,256]{2,0,1:T(8,128)(2,1)}), bf16[128,32,256]{2,0,1:T(8,128)(2,1)S(1)}, u32[]{:S(2)}, u32[]{:S(2)}) async-start(bf16[128,32,256]{2,0,1:T(8,128)(2,1)} %bitcast.108), calls=%async_computation | async-start | bytes 4194304 | tf_op jit(solution)/shard_map/all_to_all | solution.py:134
  24.8 0.1 reshape.380
  24.9 4.1 %copy.68 = bf16[128,8192]{0,1:T(8,128)(2,1)} copy(bf16[128,8192]{1,0:T(8,128)(2,1)} %param.11) | data formatting | bytes 4194304 | tf_op args[0]
  28.9 4.1 %copy.70 = bf16[1,128,64,128]{3,1,2,0:T(8,128)(2,1)} copy(bf16[1,128,64,128]{1,3,2,0:T(8,128)(2,1)} %bitcast.110) | data formatting | bytes 4194304 | tf_op jit(solution)/shard_map/reshape | solution.py:129
  33.1 3.7 %gather_fusion.5 = bf16[64,128,128]{2,1,0:T(8,128)(2,1)} fusion(bf16[1,128,64,128]{3,1,2,0:T(8,128)(2,1)} %copy.70, s32[64]{0:T(128)S(1)} %fusion.52), kind=kCustom, calls=%fused_computation.5 | custom fusion | bytes 4194816 | tf_op jit(solution)/shard_map/gather | solution.py:130
  36.8 3.2 %copy.71 = bf16[2,32,128,128]{3,2,0,1:T(8,128)(2,1)} copy(bf16[2,32,128,128]{3,2,1,0:T(8,128)(2,1)} %bitcast.109) | data formatting | bytes 4194304 | tf_op jit(solution)/shard_map/reshape | solution.py:130
  40.0 33.2 %all-to-all-done = bf16[128,32,256]{2,0,1:T(8,128)(2,1)S(1)} async-done(((bf16[128,32,256]{2,0,1:T(8,128)(2,1)}), bf16[128,32,256]{2,0,1:T(8,128)(2,1)S(1)}, u32[]{:S(2)}, u32[]{:S(2)}) %all-to-all-start) | async-done | bytes 2097184 | tf_op jit(solution)/shard_map/all_to_all | solution.py:134
  73.2 6.7 %all-to-all-start.1 = ((bf16[2,32,128,128]{3,2,0,1:T(8,128)(2,1)}), bf16[2,32,128,128]{3,2,0,1:T(8,128)(2,1)}, u32[]{:S(2)}, u32[]{:S(2)}) async-start(bf16[2,32,128,128]{3,2,0,1:T(8,128)(2,1)} %copy.71), calls=%async_computation.1 | async-start | bytes 4194304 | tf_op jit(solution)/shard_map/all_to_all | solution.py:131
  80.0 0.1 copy.65
  80.1 0.1 copy.64
  80.2 0.1 fusion.53
  80.3 0.6 gather_fusion.3
  80.9 0.6 gather_fusion.2
  81.4 0.1 copy.73
  81.5 0.1 copy.75
  81.7 0.1 fusion.43
  81.8 0.6 reduce_max.39
  82.5 0.1 fusion.44
  82.6 0.7 reduce_max.40
  83.8 5.1 %collective-permute-start = (bf16[128,256]{1,0:T(8,128)(2,1)S(1)}, bf16[128,256]{1,0:T(8,128)(2,1)S(1)}, u32[]{:S(2)}, u32[]{:S(2)}) collective-permute-start(bf16[128,256]{1,0:T(8,128)(2,1)S(1)} %slice_bitcast_fusion.4), channel_id=1, source_target_pairs={{0,32},{32,64},{64,96},{96,128},{128,160},{160,192},{192,224},{224... | collective-permute-start | bytes 196616 | tf_op jit(solution)/shard_map/ppermute | solution.py:19
  88.9 38.2 %all-to-all-done.1 = bf16[2,32,128,128]{3,2,0,1:T(8,128)(2,1)} async-done(((bf16[2,32,128,128]{3,2,0,1:T(8,128)(2,1)}), bf16[2,32,128,128]{3,2,0,1:T(8,128)(2,1)}, u32[]{:S(2)}, u32[]{:S(2)}) %all-to-all-start.1) | async-done | bytes 2097184 | tf_op jit(solution)/shard_map/all_to_all | solution.py:131
  127.1 3.2 %copy.72 = bf16[2,32,128,128]{3,2,1,0:T(8,128)(2,1)} copy(bf16[2,32,128,128]{3,2,0,1:T(8,128)(2,1)} %all-to-all-done.1) | data formatting | bytes 4194304 | tf_op jit(solution)/shard_map/all_to_all | solution.py:131
  130.3 1.7 pad_maximum_fusion
  132.1 0.6 gather_fusion.6
  132.6 0.7 broadcast_select_fusion.4
  133.4 2.5 broadcast_in_dim.93
  135.9 30.1 %while.34 = (s32[]{:T(128)}, f32[2,64,64]{2,1,0:T(8,128)S(1)}, f32[2,64,64]{2,1,0:T(8,128)S(1)}, f32[2,64,64,128]{3,2,1,0:T(8,128)}, s32[]{:T(128)}, /*index=5*/...) while((s32[]{:T(128)}, f32[2,64,64]{2,1,0:T(8,128)S(1)}, ...), condition=%wide.region_6.7_spmd.clone, body=%wide.region_2.6_spmd.clone.sunk | while | flops 277900800 | bytes 48851412 | solution.py:107
  136.0 0.1 compare_reduce_fusion.2
  136.2 0.1 reshape.560
  136.3 2.8 gather_fusion
  139.1 3.5 %fusion.73 = (f32[2,64,64]{2,1,0:T(8,128)S(1)}, f32[2,64,64,64]{3,2,1,0:T(8,128)S(1)}) fusion(pred[64,64]{0,1:T(8,128)(4,1)S(1)} %fusion.70, pred[2,64]{1,0:T(4,128)(4,1)S(1)} %and_or_fusion.2, bf16[2,64,64,128]{3,2,1,0:T(8,128)(2,1)} %get-tuple-element.741, bf16[2,64,64,256]{3,2,1,0:T(8,128)(2,1)} %bitcast.103), kind=kOutput, calls=%fused_computation.13.clone.1 | convolution fusion | flops 136306688 | bytes 6328448 | tf_op jit(solution)/shard_map/while/body/inqd,inkd->inqk/dot_general | solution.py:74
  142.6 1.4 fusion.74
  144.0 0.8 copy-done
  144.8 6.1 %multiply_add_fusion.9 = f32[2,64,64,128]{3,2,1,0:T(8,128)} fusion(f32[2,64,64,128]{3,2,1,0:T(8,128)} %get-tuple-element.719, f32[2,64,64,64]{3,2,1,0:T(8,128)S(1)} %get-tuple-element.679, bf16[2,64,64,256]{3,2,1,0:T(8,128)(2,1)S(1)} %bitcast.104, f32[2,64,64]{2,1,0:T(8,128)S(1)} %get-tuple-element.681, f32[2,64,64]{2,1,0:T(8,128)S(1)} %max.42, ...), kind=kOutput, calls=%fused_computation.16.clone.1 | convolution fusion | flops 138936320 | bytes 14819840 | tf_op jit(solution)/shard_map/while/body/inqk,inkd->inqd/dot_general | solution.py:82
  151.0 0.1 compare_reduce_fusion.2
  151.4 2.8 gather_fusion
  154.2 3.5 %fusion.73 = (f32[2,64,64]{2,1,0:T(8,128)S(1)}, f32[2,64,64,64]{3,2,1,0:T(8,128)S(1)}) fusion(pred[64,64]{0,1:T(8,128)(4,1)S(1)} %fusion.70, pred[2,64]{1,0:T(4,128)(4,1)S(1)} %and_or_fusion.2, bf16[2,64,64,128]{3,2,1,0:T(8,128)(2,1)} %get-tuple-element.741, bf16[2,64,64,256]{3,2,1,0:T(8,128)(2,1)} %bitcast.103), kind=kOutput, calls=%fused_computation.13.clone.1 | convolution fusion | flops 136306688 | bytes 6328448 | tf_op jit(solution)/shard_map/while/body/inqd,inkd->inqk/dot_general | solution.py:74
  157.7 1.4 fusion.74
  159.1 0.8 copy-done
  159.9 6.1 %multiply_add_fusion.9 = f32[2,64,64,128]{3,2,1,0:T(8,128)} fusion(f32[2,64,64,128]{3,2,1,0:T(8,128)} %get-tuple-element.719, f32[2,64,64,64]{3,2,1,0:T(8,128)S(1)} %get-tuple-element.679, bf16[2,64,64,256]{3,2,1,0:T(8,128)(2,1)S(1)} %bitcast.104, f32[2,64,64]{2,1,0:T(8,128)S(1)} %get-tuple-element.681, f32[2,64,64]{2,1,0:T(8,128)S(1)} %max.42, ...), kind=kOutput, calls=%fused_computation.16.clone.1 | convolution fusion | flops 138936320 | bytes 14819840 | tf_op jit(solution)/shard_map/while/body/inqk,inkd->inqd/dot_general | solution.py:82
  166.0 81.9 %all-reduce.3.cloned.1.call-done = bf16[8,64,256]{2,1,0:T(8,128)(2,1)} async-done(((bf16[8,64,256]{2,1,0:T(8,128)(2,1)}), bf16[8,64,256]{2,1,0:T(8,128)(2,1)}) %all-reduce.3.cloned.1.call-update) | async-done | bytes 262160 | tf_op jit(solution)/shard_map/psum | solution.py:24
  247.9 53.7 %while.35 = (s32[]{:T(128)}, f32[2,64,64]{2,1,0:T(8,128)S(1)}, f32[2,64,64]{2,1,0:T(8,128)S(1)}, f32[2,64,64,128]{3,2,1,0:T(8,128)}, s32[]{:T(128)}, /*index=5*/...) while((s32[]{:T(128)}, f32[2,64,64]{2,1,0:T(8,128)S(1)}, ...), condition=%wide.region_13.15_spmd.clone, body=%wide.region_10.14_spmd.clone.sunk | while | flops 276317728 | bytes 19667008 | solution.py:108
  248.6 1.5 gather_fusion.1
  250.1 3.7 %select_reduce_fusion.2 = (f32[2,64,64]{2,1,0:T(8,128)S(1)}, f32[2,64,64,64]{3,1,2,0:T(8,128)S(1)}) fusion(pred[2,64]{1,0:T(4,128)(4,1)S(1)} %compare_and_fusion.2, bf16[2,64,64,128]{3,2,1,0:T(8,128)(2,1)} %get-tuple-element.787, bf16[2,64,256]{2,1,0:T(8,128)(2,1)S(1)} %gather_fusion.1), kind=kOutput, calls=%fused_computation.51.clone.1 | convolution fusion | flops 135782400 | bytes 4260352 | tf_op jit(solution)/shard_map/while/body/inqd,ikd->inqk/dot_general | solution.py:94
  253.9 1.1 bitcast_reduce_fusion.2
  255.0 6.1 %multiply_add_fusion.11 = f32[2,64,64,128]{3,2,1,0:T(8,128)} fusion(f32[2,64,64,128]{3,2,1,0:T(8,128)} %get-tuple-element.767, f32[2,64,64,64]{3,1,2,0:T(8,128)S(1)} %get-tuple-element.697, f32[2,64,64]{2,1,0:T(8,128)S(1)} %get-tuple-element.699, f32[2,64,64]{2,1,0:T(8,128)S(1)} %max.43, pred[2,64]{1,0:T(4,128)(4,1)S(1)} %compare_and_fusion.2, ...), kind=kOutput, calls=%fused_computation.49.clone.1 | convolution fusion | flops 138412032 | bytes 12747264 | tf_op jit(solution)/shard_map/while/body/inqk,ikd->inqd/dot_general | solution.py:102
  261.9 1.5 gather_fusion.1
  263.4 3.7 %select_reduce_fusion.2 = (f32[2,64,64]{2,1,0:T(8,128)S(1)}, f32[2,64,64,64]{3,1,2,0:T(8,128)S(1)}) fusion(pred[2,64]{1,0:T(4,128)(4,1)S(1)} %compare_and_fusion.2, bf16[2,64,64,128]{3,2,1,0:T(8,128)(2,1)} %get-tuple-element.787, bf16[2,64,256]{2,1,0:T(8,128)(2,1)S(1)} %gather_fusion.1), kind=kOutput, calls=%fused_computation.51.clone.1 | convolution fusion | flops 135782400 | bytes 4260352 | tf_op jit(solution)/shard_map/while/body/inqd,ikd->inqk/dot_general | solution.py:94
  267.2 1.1 bitcast_reduce_fusion.2
  268.3 6.1 %multiply_add_fusion.11 = f32[2,64,64,128]{3,2,1,0:T(8,128)} fusion(f32[2,64,64,128]{3,2,1,0:T(8,128)} %get-tuple-element.767, f32[2,64,64,64]{3,1,2,0:T(8,128)S(1)} %get-tuple-element.697, f32[2,64,64]{2,1,0:T(8,128)S(1)} %get-tuple-element.699, f32[2,64,64]{2,1,0:T(8,128)S(1)} %max.43, pred[2,64]{1,0:T(4,128)(4,1)S(1)} %compare_and_fusion.2, ...), kind=kOutput, calls=%fused_computation.49.clone.1 | convolution fusion | flops 138412032 | bytes 12747264 | tf_op jit(solution)/shard_map/while/body/inqk,ikd->inqd/dot_general | solution.py:102
  275.1 1.5 gather_fusion.1
  276.7 3.7 %select_reduce_fusion.2 = (f32[2,64,64]{2,1,0:T(8,128)S(1)}, f32[2,64,64,64]{3,1,2,0:T(8,128)S(1)}) fusion(pred[2,64]{1,0:T(4,128)(4,1)S(1)} %compare_and_fusion.2, bf16[2,64,64,128]{3,2,1,0:T(8,128)(2,1)} %get-tuple-element.787, bf16[2,64,256]{2,1,0:T(8,128)(2,1)S(1)} %gather_fusion.1), kind=kOutput, calls=%fused_computation.51.clone.1 | convolution fusion | flops 135782400 | bytes 4260352 | tf_op jit(solution)/shard_map/while/body/inqd,ikd->inqk/dot_general | solution.py:94
  280.4 1.1 bitcast_reduce_fusion.2
  281.6 6.1 %multiply_add_fusion.11 = f32[2,64,64,128]{3,2,1,0:T(8,128)} fusion(f32[2,64,64,128]{3,2,1,0:T(8,128)} %get-tuple-element.767, f32[2,64,64,64]{3,1,2,0:T(8,128)S(1)} %get-tuple-element.697, f32[2,64,64]{2,1,0:T(8,128)S(1)} %get-tuple-element.699, f32[2,64,64]{2,1,0:T(8,128)S(1)} %max.43, pred[2,64]{1,0:T(4,128)(4,1)S(1)} %compare_and_fusion.2, ...), kind=kOutput, calls=%fused_computation.49.clone.1 | convolution fusion | flops 138412032 | bytes 12747264 | tf_op jit(solution)/shard_map/while/body/inqk,ikd->inqd/dot_general | solution.py:102
  288.4 1.5 gather_fusion.1
  289.9 3.7 %select_reduce_fusion.2 = (f32[2,64,64]{2,1,0:T(8,128)S(1)}, f32[2,64,64,64]{3,1,2,0:T(8,128)S(1)}) fusion(pred[2,64]{1,0:T(4,128)(4,1)S(1)} %compare_and_fusion.2, bf16[2,64,64,128]{3,2,1,0:T(8,128)(2,1)} %get-tuple-element.787, bf16[2,64,256]{2,1,0:T(8,128)(2,1)S(1)} %gather_fusion.1), kind=kOutput, calls=%fused_computation.51.clone.1 | convolution fusion | flops 135782400 | bytes 4260352 | tf_op jit(solution)/shard_map/while/body/inqd,ikd->inqk/dot_general | solution.py:94
  293.7 1.1 bitcast_reduce_fusion.2
  294.8 6.1 %multiply_add_fusion.11 = f32[2,64,64,128]{3,2,1,0:T(8,128)} fusion(f32[2,64,64,128]{3,2,1,0:T(8,128)} %get-tuple-element.767, f32[2,64,64,64]{3,1,2,0:T(8,128)S(1)} %get-tuple-element.697, f32[2,64,64]{2,1,0:T(8,128)S(1)} %get-tuple-element.699, f32[2,64,64]{2,1,0:T(8,128)S(1)} %max.43, pred[2,64]{1,0:T(4,128)(4,1)S(1)} %compare_and_fusion.2, ...), kind=kOutput, calls=%fused_computation.49.clone.1 | convolution fusion | flops 138412032 | bytes 12747264 | tf_op jit(solution)/shard_map/while/body/inqk,ikd->inqd/dot_general | solution.py:102
  301.5 3.8 %divide_convert_fusion = bf16[2,64,64,128]{3,2,1,0:T(8,128)(2,1)} fusion(f32[2,64,64,128]{3,2,1,0:T(8,128)} %get-tuple-element.217, f32[2,64,64]{2,1,0:T(8,128)S(1)} %get-tuple-element.218), kind=kLoop, calls=%fused_computation.72 | loop fusion | flops 2097152 | bytes 6324224 | tf_op jit(solution)/shard_map/convert_element_type | solution.py:110
  (75 shorter events, 1.7 us)
Async XLA Ops:
  11.0 62.2 %all-to-all-start = ((bf16[128,32,256]{2,0,1:T(8,128)(2,1)}), bf16[128,32,256]{2,0,1:T(8,128)(2,1)S(1)}, u32[]{:S(2)}, u32[]{:S(2)}) async-start(bf16[128,32,256]{2,0,1:T(8,128)(2,1)} %bitcast.108), calls=%async_computation | async-start | bytes 4194304 | tf_op jit(solution)/shard_map/all_to_all | solution.py:134
  36.8 43.2 %copy-start.2 = (s32[64,4]{0,1:T(4,128)S(1)}, s32[64,4]{0,1:T(4,128)}, u32[]{:S(2)}) copy-start(s32[64,4]{0,1:T(4,128)} %param.13) | copy-start | bytes 3076
  36.8 43.3 %copy-start.4 = (s32[64,2]{0,1:T(2,128)S(1)}, s32[64,2]{0,1:T(2,128)}, u32[]{:S(2)}) copy-start(s32[64,2]{0,1:T(2,128)} %param.14) | copy-start | bytes 1540
  36.8 43.4 %copy-start.3 = (s32[64]{0:T(128)S(1)}, s32[64]{0:T(128)}, u32[]{:S(2)}) copy-start(s32[64]{0:T(128)} %param.15) | copy-start | bytes 772
  73.2 57.2 %copy-start.1 = (bf16[128,32,256]{2,0,1:T(8,128)(2,1)}, bf16[128,32,256]{2,0,1:T(8,128)(2,1)S(1)}, u32[]{:S(2)}) copy-start(bf16[128,32,256]{2,0,1:T(8,128)(2,1)S(1)} %all-to-all-done) | copy-start | bytes 6291460
  73.2 53.9 %all-to-all-start.1 = ((bf16[2,32,128,128]{3,2,0,1:T(8,128)(2,1)}), bf16[2,32,128,128]{3,2,0,1:T(8,128)(2,1)}, u32[]{:S(2)}, u32[]{:S(2)}) async-start(bf16[2,32,128,128]{3,2,0,1:T(8,128)(2,1)} %copy.71), calls=%async_computation.1 | async-start | bytes 4194304 | tf_op jit(solution)/shard_map/all_to_all | solution.py:131
  79.9 167.9 %all-reduce.3.cloned.1.call-start = ((), (), s32[]{:S(2)}) async-start(), calls=%async_computation.2 | async-start | bytes 524288 | tf_op jit(solution)/shard_map/psum | solution.py:24
  83.8 46.5 %collective-permute-start = (bf16[128,256]{1,0:T(8,128)(2,1)S(1)}, bf16[128,256]{1,0:T(8,128)(2,1)S(1)}, u32[]{:S(2)}, u32[]{:S(2)}) collective-permute-start(bf16[128,256]{1,0:T(8,128)(2,1)S(1)} %slice_bitcast_fusion.4), channel_id=1, source_target_pairs={{0,32},{32,64},{64,96},{96,128},{128,160},{160,192},{192,224},{224... | collective-permute-start | bytes 196616 | tf_op jit(solution)/shard_map/ppermute | solution.py:19
  142.6 2.2 copy-start
  157.6 2.2 copy-start
Sparse Core Ops, SparseCore 0:
  133.5 114.2 all-reduce.2
where the time goes:
time: 314 us; the launch traced here: 312 us
  waiting for transfers between devices  153 us (49%)
  matrix products  58.4 us (19%)
  local copies, waits for them, and re-layouts  40.7 us (13%)
  starting transfers between devices  25.6 us (8%)
  other arithmetic  16.7 us (5%)
  between operations  14.1 us (4%)
  loops' own time  3.48 us (1%)
    psum x1, waiting for transfers between devices, broadcast(): return lax.psum(block, axis)  81.9 us
    all_to_all x1, waiting for transfers between devices, on_device(): lax.all_to_all(outgoing, 'head', split_axis=1, concat_axis=1, tiled=True)  38.2 us
    all_to_all x1, waiting for transfers between devices, on_device(): lax.all_to_all(shipped, 'head', split_axis=1, concat_axis=0, tiled=True)  33.2 us
    dot_general x4, matrix products, vertical_step(): jnp.einsum('inqk,ikd->inqd', weights, values, preferred_element_type=jnp....  24.2 us
    dot_general x4, matrix products, vertical_step(): jnp.einsum('inqd,ikd->inqk', query_blocks, keys, preferred_element_type=j...  14.9 us
    all_to_all x1, starting transfers between devices, on_device(): lax.all_to_all(shipped, 'head', split_axis=1, concat_axis=0, tiled=True)  13.7 us
    dot_general x2, matrix products, main_step(): jnp.einsum('inqk,inkd->inqd', weights, values, preferred_element_type=jnp...  12.3 us
    reduce_sum x6, other arithmetic, softmax_update(): total = total * factor + jnp.sum(weights, axis=-1)  7.12 us
  transfers between devices with their start and end apart: 4, of which 3 were waited for; matrix products, arithmetic and copies ran while one was open for 17% of the time, Pallas kernels for 0%

commit v1 on v0

--- a/solution.py
+++ b/solution.py
@@ -21,7 +21,7 @@
 
 def broadcast(block, axis, holder):
     block = jnp.where(lax.axis_index(axis) == holder, block, jnp.zeros_like(block))
-    return lax.psum(block, axis)
+    return jnp.sum(lax.all_gather(block, axis), axis=0)
 
 
 def softmax_update(state, scores, mask, product):

time: 314 us -> 244 us (0.78)
  the two profiles are of different devices: /device:TPU:1 before, /device:TPU:4 now
where the time goes in v1:
time: 244 us; the launch traced here: 243 us
  waiting for transfers between devices  78.7 us (32%)
  matrix products  62.5 us (26%)
  local copies, waits for them, and re-layouts  40.9 us (17%)
  other arithmetic  21.7 us (9%)
  starting transfers between devices  21.1 us (9%)
  between operations  14.3 us (6%)
  loops' own time  3.53 us (1%)
    all_to_all x1, waiting for transfers between devices, on_device(): lax.all_to_all(outgoing, 'head', split_axis=1, concat_axis=1, tiled=True)  44.2 us
    all_to_all x1, waiting for transfers between devices, on_device(): lax.all_to_all(shipped, 'head', split_axis=1, concat_axis=0, tiled=True)  34.5 us
    dot_general x4, matrix products, vertical_step(): jnp.einsum('inqk,ikd->inqd', weights, values, preferred_element_type=jnp....  24.2 us
    dot_general x3, matrix products, main_step(): jnp.einsum('inqk,inkd->inqd', weights, values, preferred_element_type=jnp...  18.4 us
    all_to_all x1, starting transfers between devices, on_device(): lax.all_to_all(shipped, 'head', split_axis=1, concat_axis=0, tiled=True)  13.4 us
    dot_general x3, matrix products, main_step(): jnp.einsum('inqd,inkd->inqk', query_blocks, keys, preferred_element_type=...  10.5 us
    dot_general x4, matrix products, vertical_step(): jnp.einsum('inqd,ikd->inqk', query_blocks, keys, preferred_element_type=j...  9.29 us
    reduce_sum x7, other arithmetic, softmax_update(): total = total * factor + jnp.sum(weights, axis=-1)  8.47 us
  transfers between devices with their start and end apart: 4, of which 2 were waited for; matrix products, arithmetic and copies ran while one was open for 28% of the time, Pallas kernels for 0%

profile of v1, /device:TPU:4, one launch (start us, length us, event | category | flops | bytes accessed | tf_op | source)
XLA Modules:
  0.0 242.6 jit_solution(312857676653968808)
XLA Ops:
  6.5 0.7 reshape.388
  7.3 0.1 fusion.41
  7.4 1.3 copy.66
  8.8 0.2 copy.67
  9.0 2.0 gather_fusion.4
  11.0 13.4 %all-to-all-start = ((bf16[128,32,256]{2,0,1:T(8,128)(2,1)}), bf16[128,32,256]{2,0,1:T(8,128)(2,1)S(1)}, u32[]{:S(2)}, u32[]{:S(2)}) async-start(bf16[128,32,256]{2,0,1:T(8,128)(2,1)} %bitcast.111), calls=%async_computation | async-start | bytes 4194304 | tf_op jit(solution)/shard_map/all_to_all | solution.py:134
  24.6 4.1 %copy.68 = bf16[128,8192]{0,1:T(8,128)(2,1)} copy(bf16[128,8192]{1,0:T(8,128)(2,1)} %param.11) | data formatting | bytes 4194304 | tf_op args[0]
  28.7 4.1 %copy.70 = bf16[1,128,64,128]{3,1,2,0:T(8,128)(2,1)} copy(bf16[1,128,64,128]{1,3,2,0:T(8,128)(2,1)} %bitcast.113) | data formatting | bytes 4194304 | tf_op jit(solution)/shard_map/reshape | solution.py:129
  32.8 3.7 %gather_fusion.5 = bf16[64,128,128]{2,1,0:T(8,128)(2,1)} fusion(bf16[1,128,64,128]{3,1,2,0:T(8,128)(2,1)} %copy.70, s32[64]{0:T(128)S(1)} %fusion.52), kind=kCustom, calls=%fused_computation.5 | custom fusion | bytes 4194816 | tf_op jit(solution)/shard_map/gather | solution.py:130
  36.5 3.2 %copy.71 = bf16[2,32,128,128]{3,2,0,1:T(8,128)(2,1)} copy(bf16[2,32,128,128]{3,2,1,0:T(8,128)(2,1)} %bitcast.112) | data formatting | bytes 4194304 | tf_op jit(solution)/shard_map/reshape | solution.py:130
  39.7 34.5 %all-to-all-done = bf16[128,32,256]{2,0,1:T(8,128)(2,1)S(1)} async-done(((bf16[128,32,256]{2,0,1:T(8,128)(2,1)}), bf16[128,32,256]{2,0,1:T(8,128)(2,1)S(1)}, u32[]{:S(2)}, u32[]{:S(2)}) %all-to-all-start) | async-done | bytes 2097184 | tf_op jit(solution)/shard_map/all_to_all | solution.py:134
  74.2 6.3 %all-to-all-start.1 = ((bf16[2,32,128,128]{3,2,0,1:T(8,128)(2,1)}), bf16[2,32,128,128]{3,2,0,1:T(8,128)(2,1)}, u32[]{:S(2)}, u32[]{:S(2)}) async-start(bf16[2,32,128,128]{3,2,0,1:T(8,128)(2,1)} %copy.71), calls=%async_computation.1 | async-start | bytes 4194304 | tf_op jit(solution)/shard_map/all_to_all | solution.py:131
  80.7 0.1 copy.65
  80.8 0.1 copy.64
  81.0 0.6 gather_fusion.3
  81.5 0.6 gather_fusion.2
  82.1 0.1 copy.73
  82.2 0.1 copy.75
  82.4 0.1 fusion.43
  82.5 0.7 reduce_max.39
  83.2 0.1 fusion.44
  83.3 0.7 reduce_max.40
  84.7 1.3 collective-permute-start
  86.1 44.2 %all-to-all-done.1 = bf16[2,32,128,128]{3,2,0,1:T(8,128)(2,1)} async-done(((bf16[2,32,128,128]{3,2,0,1:T(8,128)(2,1)}), bf16[2,32,128,128]{3,2,0,1:T(8,128)(2,1)}, u32[]{:S(2)}, u32[]{:S(2)}) %all-to-all-start.1) | async-done | bytes 2097184 | tf_op jit(solution)/shard_map/all_to_all | solution.py:131
  130.2 3.2 %copy.72 = bf16[2,32,128,128]{3,2,1,0:T(8,128)(2,1)} copy(bf16[2,32,128,128]{3,2,0,1:T(8,128)(2,1)} %all-to-all-done.1) | data formatting | bytes 4194304 | tf_op jit(solution)/shard_map/all_to_all | solution.py:131
  133.4 1.7 pad_maximum_fusion
  135.1 0.6 gather_fusion.6
  135.7 0.7 broadcast_select_fusion.4
  136.5 2.5 %broadcast_in_dim.93 = f32[2,64,64,128]{3,2,1,0:T(8,128)} broadcast(f32[]{:T(128)} %constant.207.clone.1), dimensions={} | broadcast | bytes 4194308 | tf_op jit(solution)/shard_map/broadcast_in_dim | solution.py:61
  139.0 45.6 %while.34 = (s32[]{:T(128)}, f32[2,64,64]{2,1,0:T(8,128)S(1)}, f32[2,64,64]{2,1,0:T(8,128)S(1)}, f32[2,64,64,128]{3,2,1,0:T(8,128)}, s32[]{:T(128)}, /*index=5*/...) while((s32[]{:T(128)}, f32[2,64,64]{2,1,0:T(8,128)S(1)}, ...), condition=%wide.region_6.7_spmd.clone, body=%wide.region_2.6_spmd.clone.sunk | while | flops 277900800 | bytes 48851412 | solution.py:107
  139.4 2.8 %gather_fusion = bf16[128,64,256]{2,1,0:T(8,128)(2,1)} fusion(bf16[66,64,1,256]{3,1,2,0:T(8,128)(2,1)S(1)} %get-tuple-element.738, s32[128]{0:T(128)S(1)} %reshape.570), kind=kCustom, calls=%fused_computation.clone.clone.1 | custom fusion | bytes 8389632 | tf_op jit(solution)/shard_map/while/body/gather | solution.py:70
  142.3 3.5 %fusion.73 = (f32[2,64,64]{2,1,0:T(8,128)S(1)}, f32[2,64,64,64]{3,2,1,0:T(8,128)S(1)}) fusion(pred[64,64]{0,1:T(8,128)(4,1)S(1)} %fusion.70, pred[2,64]{1,0:T(4,128)(4,1)S(1)} %and_or_fusion.2, bf16[2,64,64,128]{3,2,1,0:T(8,128)(2,1)} %get-tuple-element.739, bf16[2,64,64,256]{3,2,1,0:T(8,128)(2,1)} %bitcast.106), kind=kOutput, calls=%fused_computation.13.clone.1 | convolution fusion | flops 136306688 | bytes 6328448 | tf_op jit(solution)/shard_map/while/body/inqd,inkd->inqk/dot_general | solution.py:74
  145.8 1.4 fusion.74
  147.2 0.9 copy-done
  148.1 6.1 %multiply_add_fusion.9 = f32[2,64,64,128]{3,2,1,0:T(8,128)} fusion(f32[2,64,64,128]{3,2,1,0:T(8,128)} %get-tuple-element.717, f32[2,64,64,64]{3,2,1,0:T(8,128)S(1)} %get-tuple-element.677, bf16[2,64,64,256]{3,2,1,0:T(8,128)(2,1)S(1)} %bitcast.107, f32[2,64,64]{2,1,0:T(8,128)S(1)} %get-tuple-element.679, f32[2,64,64]{2,1,0:T(8,128)S(1)} %max.42, ...), kind=kOutput, calls=%fused_computation.16.clone.1 | convolution fusion | flops 138936320 | bytes 14819840 | tf_op jit(solution)/shard_map/while/body/inqk,inkd->inqd/dot_general | solution.py:82
  154.6 2.8 %gather_fusion = bf16[128,64,256]{2,1,0:T(8,128)(2,1)} fusion(bf16[66,64,1,256]{3,1,2,0:T(8,128)(2,1)S(1)} %get-tuple-element.738, s32[128]{0:T(128)S(1)} %reshape.570), kind=kCustom, calls=%fused_computation.clone.clone.1 | custom fusion | bytes 8389632 | tf_op jit(solution)/shard_map/while/body/gather | solution.py:70
  157.5 3.5 %fusion.73 = (f32[2,64,64]{2,1,0:T(8,128)S(1)}, f32[2,64,64,64]{3,2,1,0:T(8,128)S(1)}) fusion(pred[64,64]{0,1:T(8,128)(4,1)S(1)} %fusion.70, pred[2,64]{1,0:T(4,128)(4,1)S(1)} %and_or_fusion.2, bf16[2,64,64,128]{3,2,1,0:T(8,128)(2,1)} %get-tuple-element.739, bf16[2,64,64,256]{3,2,1,0:T(8,128)(2,1)} %bitcast.106), kind=kOutput, calls=%fused_computation.13.clone.1 | convolution fusion | flops 136306688 | bytes 6328448 | tf_op jit(solution)/shard_map/while/body/inqd,inkd->inqk/dot_general | solution.py:74
  161.0 1.4 fusion.74
  162.4 0.9 copy-done
  163.3 6.2 %multiply_add_fusion.9 = f32[2,64,64,128]{3,2,1,0:T(8,128)} fusion(f32[2,64,64,128]{3,2,1,0:T(8,128)} %get-tuple-element.717, f32[2,64,64,64]{3,2,1,0:T(8,128)S(1)} %get-tuple-element.677, bf16[2,64,64,256]{3,2,1,0:T(8,128)(2,1)S(1)} %bitcast.107, f32[2,64,64]{2,1,0:T(8,128)S(1)} %get-tuple-element.679, f32[2,64,64]{2,1,0:T(8,128)S(1)} %max.42, ...), kind=kOutput, calls=%fused_computation.16.clone.1 | convolution fusion | flops 138936320 | bytes 14819840 | tf_op jit(solution)/shard_map/while/body/inqk,inkd->inqd/dot_general | solution.py:82
  169.9 2.8 %gather_fusion = bf16[128,64,256]{2,1,0:T(8,128)(2,1)} fusion(bf16[66,64,1,256]{3,1,2,0:T(8,128)(2,1)S(1)} %get-tuple-element.738, s32[128]{0:T(128)S(1)} %reshape.570), kind=kCustom, calls=%fused_computation.clone.clone.1 | custom fusion | bytes 8389632 | tf_op jit(solution)/shard_map/while/body/gather | solution.py:70
  172.7 3.6 %fusion.73 = (f32[2,64,64]{2,1,0:T(8,128)S(1)}, f32[2,64,64,64]{3,2,1,0:T(8,128)S(1)}) fusion(pred[64,64]{0,1:T(8,128)(4,1)S(1)} %fusion.70, pred[2,64]{1,0:T(4,128)(4,1)S(1)} %and_or_fusion.2, bf16[2,64,64,128]{3,2,1,0:T(8,128)(2,1)} %get-tuple-element.739, bf16[2,64,64,256]{3,2,1,0:T(8,128)(2,1)} %bitcast.106), kind=kOutput, calls=%fused_computation.13.clone.1 | convolution fusion | flops 136306688 | bytes 6328448 | tf_op jit(solution)/shard_map/while/body/inqd,inkd->inqk/dot_general | solution.py:74
  176.3 1.4 fusion.74
  177.7 0.8 copy-done
  178.4 6.1 %multiply_add_fusion.9 = f32[2,64,64,128]{3,2,1,0:T(8,128)} fusion(f32[2,64,64,128]{3,2,1,0:T(8,128)} %get-tuple-element.717, f32[2,64,64,64]{3,2,1,0:T(8,128)S(1)} %get-tuple-element.677, bf16[2,64,64,256]{3,2,1,0:T(8,128)(2,1)S(1)} %bitcast.107, f32[2,64,64]{2,1,0:T(8,128)S(1)} %get-tuple-element.679, f32[2,64,64]{2,1,0:T(8,128)S(1)} %max.42, ...), kind=kOutput, calls=%fused_computation.16.clone.1 | convolution fusion | flops 138936320 | bytes 14819840 | tf_op jit(solution)/shard_map/while/body/inqk,inkd->inqd/dot_general | solution.py:82
  184.6 3.1 %reduce_sum.53 = bf16[2,4,64,256]{3,2,1,0:T(8,128)(2,1)S(1)} reduce(bf16[16,2,4,64,256]{4,3,2,1,0:T(8,128)(2,1)} %bitcast.114, bf16[]{:T(256)} %constant.224.clone.1), dimensions={0}, to_apply=%region_9.10 | reduce | flops 1966080 | bytes 4456450 | tf_op jit(solution)/shard_map/reduce_sum | solution.py:24
  187.7 44.2 %while.35 = (s32[]{:T(128)}, f32[2,64,64]{2,1,0:T(8,128)S(1)}, f32[2,64,64]{2,1,0:T(8,128)S(1)}, f32[2,64,64,128]{3,2,1,0:T(8,128)}, s32[]{:T(128)}, /*index=5*/...) while((s32[]{:T(128)}, f32[2,64,64]{2,1,0:T(8,128)S(1)}, ...), condition=%wide.region_13.15_spmd.clone, body=%wide.region_10.14_spmd.clone.sunk | while | flops 276317728 | bytes 19667008 | solution.py:108
  188.5 0.6 gather_fusion.1
  189.1 2.3 select_reduce_fusion.2
  191.4 1.1 bitcast_reduce_fusion.2
  192.6 6.0 %multiply_add_fusion.11 = f32[2,64,64,128]{3,2,1,0:T(8,128)} fusion(f32[2,64,64,128]{3,2,1,0:T(8,128)} %get-tuple-element.765, f32[2,64,64,64]{3,1,2,0:T(8,128)S(1)} %get-tuple-element.695, f32[2,64,64]{2,1,0:T(8,128)S(1)} %get-tuple-element.697, f32[2,64,64]{2,1,0:T(8,128)S(1)} %max.43, pred[2,64]{1,0:T(4,128)(4,1)S(1)} %compare_and_fusion.2, ...), kind=kOutput, calls=%fused_computation.49.clone.1 | convolution fusion | flops 138412032 | bytes 12747264 | tf_op jit(solution)/shard_map/while/body/inqk,ikd->inqd/dot_general | solution.py:102
  199.4 0.6 gather_fusion.1
  200.0 2.3 select_reduce_fusion.2
  202.3 1.1 bitcast_reduce_fusion.2
  203.5 6.0 %multiply_add_fusion.11 = f32[2,64,64,128]{3,2,1,0:T(8,128)} fusion(f32[2,64,64,128]{3,2,1,0:T(8,128)} %get-tuple-element.765, f32[2,64,64,64]{3,1,2,0:T(8,128)S(1)} %get-tuple-element.695, f32[2,64,64]{2,1,0:T(8,128)S(1)} %get-tuple-element.697, f32[2,64,64]{2,1,0:T(8,128)S(1)} %max.43, pred[2,64]{1,0:T(4,128)(4,1)S(1)} %compare_and_fusion.2, ...), kind=kOutput, calls=%fused_computation.49.clone.1 | convolution fusion | flops 138412032 | bytes 12747264 | tf_op jit(solution)/shard_map/while/body/inqk,ikd->inqd/dot_general | solution.py:102
  210.3 0.6 gather_fusion.1
  210.9 2.3 select_reduce_fusion.2
  213.2 1.1 bitcast_reduce_fusion.2
  214.4 6.0 %multiply_add_fusion.11 = f32[2,64,64,128]{3,2,1,0:T(8,128)} fusion(f32[2,64,64,128]{3,2,1,0:T(8,128)} %get-tuple-element.765, f32[2,64,64,64]{3,1,2,0:T(8,128)S(1)} %get-tuple-element.695, f32[2,64,64]{2,1,0:T(8,128)S(1)} %get-tuple-element.697, f32[2,64,64]{2,1,0:T(8,128)S(1)} %max.43, pred[2,64]{1,0:T(4,128)(4,1)S(1)} %compare_and_fusion.2, ...), kind=kOutput, calls=%fused_computation.49.clone.1 | convolution fusion | flops 138412032 | bytes 12747264 | tf_op jit(solution)/shard_map/while/body/inqk,ikd->inqd/dot_general | solution.py:102
  221.2 0.6 gather_fusion.1
  221.8 2.3 select_reduce_fusion.2
  224.1 1.1 bitcast_reduce_fusion.2
  225.3 6.0 %multiply_add_fusion.11 = f32[2,64,64,128]{3,2,1,0:T(8,128)} fusion(f32[2,64,64,128]{3,2,1,0:T(8,128)} %get-tuple-element.765, f32[2,64,64,64]{3,1,2,0:T(8,128)S(1)} %get-tuple-element.695, f32[2,64,64]{2,1,0:T(8,128)S(1)} %get-tuple-element.697, f32[2,64,64]{2,1,0:T(8,128)S(1)} %max.43, pred[2,64]{1,0:T(4,128)(4,1)S(1)} %compare_and_fusion.2, ...), kind=kOutput, calls=%fused_computation.49.clone.1 | convolution fusion | flops 138412032 | bytes 12747264 | tf_op jit(solution)/shard_map/while/body/inqk,ikd->inqd/dot_general | solution.py:102
  232.0 3.8 %divide_convert_fusion = bf16[2,64,64,128]{3,2,1,0:T(8,128)(2,1)} fusion(f32[2,64,64,128]{3,2,1,0:T(8,128)} %get-tuple-element.217, f32[2,64,64]{2,1,0:T(8,128)S(1)} %get-tuple-element.218), kind=kLoop, calls=%fused_computation.72 | loop fusion | flops 2097152 | bytes 6324224 | tf_op jit(solution)/shard_map/convert_element_type | solution.py:110
  (95 shorter events, 2.7 us)
Async XLA Ops:
  11.0 63.3 %all-to-all-start = ((bf16[128,32,256]{2,0,1:T(8,128)(2,1)}), bf16[128,32,256]{2,0,1:T(8,128)(2,1)S(1)}, u32[]{:S(2)}, u32[]{:S(2)}) async-start(bf16[128,32,256]{2,0,1:T(8,128)(2,1)} %bitcast.111), calls=%async_computation | async-start | bytes 4194304 | tf_op jit(solution)/shard_map/all_to_all | solution.py:134
  36.5 44.1 %copy-start.3 = (s32[64,4]{0,1:T(4,128)S(1)}, s32[64,4]{0,1:T(4,128)}, u32[]{:S(2)}) copy-start(s32[64,4]{0,1:T(4,128)} %param.13) | copy-start | bytes 3076
  36.5 44.2 %copy-start.5 = (s32[64,2]{0,1:T(2,128)S(1)}, s32[64,2]{0,1:T(2,128)}, u32[]{:S(2)}) copy-start(s32[64,2]{0,1:T(2,128)} %param.14) | copy-start | bytes 1540
  36.5 44.3 %copy-start.4 = (s32[64]{0:T(128)S(1)}, s32[64]{0:T(128)}, u32[]{:S(2)}) copy-start(s32[64]{0:T(128)} %param.15) | copy-start | bytes 772
  74.2 59.2 %copy-start.2 = (bf16[128,32,256]{2,0,1:T(8,128)(2,1)}, bf16[128,32,256]{2,0,1:T(8,128)(2,1)S(1)}, u32[]{:S(2)}) copy-start(bf16[128,32,256]{2,0,1:T(8,128)(2,1)S(1)} %all-to-all-done) | copy-start | bytes 6291460
  74.2 56.0 %all-to-all-start.1 = ((bf16[2,32,128,128]{3,2,0,1:T(8,128)(2,1)}), bf16[2,32,128,128]{3,2,0,1:T(8,128)(2,1)}, u32[]{:S(2)}, u32[]{:S(2)}) async-start(bf16[2,32,128,128]{3,2,0,1:T(8,128)(2,1)} %copy.71), calls=%async_computation.1 | async-start | bytes 4194304 | tf_op jit(solution)/shard_map/all_to_all | solution.py:131
  80.6 104.0 %all-gather.3.cloned.1.call-start = ((), (), s32[]{:S(2)}) async-start(), calls=%async_computation.2 | async-start | bytes 4456448 | tf_op jit(solution)/shard_map/all_gather | solution.py:24
  84.7 48.7 %collective-permute-start = (bf16[128,256]{1,0:T(8,128)(2,1)S(1)}, bf16[128,256]{1,0:T(8,128)(2,1)S(1)}, u32[]{:S(2)}, u32[]{:S(2)}) collective-permute-start(bf16[128,256]{1,0:T(8,128)(2,1)S(1)} %slice_bitcast_fusion.4), channel_id=1, source_target_pairs={{0,32},{32,64},{64,96},{96,128},{128,160},{160,192},{192,224},{224... | collective-permute-start | bytes 196616 | tf_op jit(solution)/shard_map/ppermute | solution.py:19
  145.7 2.4 copy-start
  161.0 2.3 copy-start
  176.2 2.2 copy-start
  184.6 3.2 %copy-start.1 = (bf16[2,64,64,128]{3,2,1,0:T(8,128)(2,1)S(1)}, bf16[2,64,64,128]{3,2,1,0:T(8,128)(2,1)}, u32[]{:S(2)}) copy-start(bf16[2,64,64,128]{3,2,1,0:T(8,128)(2,1)} %get-tuple-element.795) | copy-start | bytes 6291460
Sparse Core Ops, SparseCore 0:
  136.6 41.5 all-gather.2
